TPU v7x, 32 devices: a whole 2x2x4 slice. The times are simulated.
32 devices in a mesh: grp: 2 (over x), seq: 16 (over z, y, core).
Axes of the slice: x: 2, y: 2, z: 4, core: 2. Of those that a mesh axis runs over, the one named last changes fastest.
Arguments:
- tokens: bfloat16 [16384, 1024], P(('grp', 'seq')), may hold values from -20 to 20
- qkv_weight: bfloat16 [1024, 1536], replicated, may hold values from -2 to 2
- cov_embed: bfloat16 [64, 1024], P(('grp', 'seq')), may hold values from -20 to 20
- cov_slot: int32 [32], replicated, may hold values from 0 to 63, as said below
- block_links: int32 [128, 2], P(('grp', 'seq')), may hold values from 0 to 1, as said below
Outputs:
- attended: bfloat16 [16384, 512], P(('grp', 'seq'))
Inputs may be any that keep to these rules, and one draw needn't show every extreme that they name: The values are distinct; covariate c is held in slot cov_slot[c], on the device that holds that row of cov_embed. block_links[b, 1] equals block_links[b + 1, 0]; block_links[0, 0] and block_links[127, 1] are 0.
All inputs are finite; a program needn't handle non-finite values.
Results may differ from a plain program's by a relative error of at most 0.0015.
The roundings to bfloat16 on the way count: a program that leaves them out, or rounds other values in their place, can miss the bound.
Values may be sent and summed in bfloat16 or wider, within the bound.
A program may use at most 64 MiB of HBM per device.

v0:
```python
import math
import jax
import jax.numpy as jnp
from jax import lax
from jax.sharding import PartitionSpec as P

HEADS = 8
BLOCK = 128
masked_score = -1e30


def extended(cells, sides, width):
    for axis, dim in sides:
        count = lax.axis_size(axis)
        ends = count - 1
        head = lax.slice_in_dim(cells, 0, width, axis=dim)
        tail = lax.slice_in_dim(cells, cells.shape[dim] - width, cells.shape[dim], axis=dim)
        cells = jnp.concatenate(
            [
                lax.ppermute(tail, axis, [(i, (i + 1) % count) for i in range(ends)]),
                cells,
                lax.ppermute(head, axis, [((i + 1) % count, i) for i in range(ends)]),
            ],
            axis=dim,
        )
    return cells


def window_attend(queries, before, middle, after, left_open, right_open, cov_kv, head_count):
    blocks, block_rows, attn_width = queries.shape
    head_width = attn_width // head_count
    score_scale = 1.0 / math.sqrt(head_width)
    query_heads = queries.reshape(blocks, block_rows, head_count, head_width)

    def divide_parts(joined):
        key_part = joined[:, :, :attn_width].reshape(blocks, block_rows, head_count, head_width)
        value_part = joined[:, :, attn_width:].reshape(blocks, block_rows, head_count, head_width)
        return (key_part, value_part)

    key_before, value_before = divide_parts(before)
    key_middle, value_middle = divide_parts(middle)
    key_after, value_after = divide_parts(after)
    cov_count = cov_kv.shape[0]
    cov_keys = cov_kv[:, :attn_width].reshape(cov_count, head_count, head_width)
    cov_values = cov_kv[:, attn_width:].reshape(cov_count, head_count, head_width)

    def local_scores(key_part):
        return (
            jnp.einsum("nqhd,nkhd->nqhk", query_heads, key_part, preferred_element_type=jnp.float32)
            * score_scale
        )

    score_before = jnp.where(
        (left_open > 0)[:, None, None, None], local_scores(key_before), masked_score
    )
    score_middle = local_scores(key_middle)
    score_after = jnp.where(
        (right_open > 0)[:, None, None, None], local_scores(key_after), masked_score
    )
    score_global = (
        jnp.einsum("nqhd,chd->nqhc", query_heads, cov_keys, preferred_element_type=jnp.float32)
        * score_scale
    )
    highest = jnp.maximum(
        jnp.maximum(
            jnp.max(score_before, axis=-1, keepdims=True),
            jnp.max(score_middle, axis=-1, keepdims=True),
        ),
        jnp.maximum(
            jnp.max(score_after, axis=-1, keepdims=True),
            jnp.max(score_global, axis=-1, keepdims=True),
        ),
    )
    weight_before = jnp.exp(score_before - highest)
    weight_middle = jnp.exp(score_middle - highest)
    weight_after = jnp.exp(score_after - highest)
    weight_global = jnp.exp(score_global - highest)
    denominator = (
        jnp.sum(weight_before, axis=-1)
        + jnp.sum(weight_middle, axis=-1)
        + jnp.sum(weight_after, axis=-1)
        + jnp.sum(weight_global, axis=-1)
    )

    def local_values(weights, value_part):
        return jnp.einsum(
            "nqhk,nkhd->nqhd",
            weights.astype(jnp.bfloat16),
            value_part,
            preferred_element_type=jnp.float32,
        )

    summed = local_values(weight_before, value_before) + local_values(weight_middle, value_middle)
    summed = summed + local_values(weight_after, value_after)
    summed = summed + jnp.einsum(
        "nqhc,chd->nqhd",
        weight_global.astype(jnp.bfloat16),
        cov_values,
        preferred_element_type=jnp.float32,
    )
    result = (summed / denominator[..., None]).astype(jnp.bfloat16)
    return result.reshape(blocks * block_rows, attn_width)


def local(tokens, qkv_weight, cov_embed, cov_slot, block_links):
    tok_rows = tokens.shape[0]
    attn_width = qkv_weight.shape[1] // 3
    block_rows = BLOCK
    blocks = tok_rows // block_rows
    projected = jnp.dot(tokens, qkv_weight, preferred_element_type=jnp.float32).astype(jnp.bfloat16)
    queries = projected[:, :attn_width]
    keyvalue = projected[:, attn_width:]
    padded = extended(keyvalue, ((("grp", "seq"), 0),), block_rows)
    value_weight = qkv_weight[:, attn_width:]
    every_row = lax.all_gather(cov_embed, ("grp", "seq"), axis=0, tiled=True)
    chosen = jnp.take(every_row, cov_slot, axis=0)
    cov_kv = jnp.dot(chosen, value_weight, preferred_element_type=jnp.float32).astype(jnp.bfloat16)
    before = padded[:tok_rows].reshape(blocks, block_rows, 2 * attn_width)
    middle = keyvalue.reshape(blocks, block_rows, 2 * attn_width)
    after = padded[2 * block_rows : 2 * block_rows + tok_rows].reshape(
        blocks, block_rows, 2 * attn_width
    )
    return window_attend(
        queries.reshape(blocks, block_rows, attn_width),
        before,
        middle,
        after,
        block_links[:, 0],
        block_links[:, 1],
        cov_kv,
        HEADS,
    )


def solution(mesh):
    placed = (P(("grp", "seq"), None), P(), P(("grp", "seq"), None), P(), P(("grp", "seq"), None))
    return jax.shard_map(
        local, mesh=mesh, in_specs=placed, out_specs=P(("grp", "seq"), None), check_vma=False
    )
```

profile of v0, /device:TPU:0, one launch (start us, length us, event | category | flops | bytes accessed | tf_op | source)
XLA Modules:
  0.0 99.4 jit_solution(9266033365159456441)
XLA Ops:
  0.0 1.2 %copy-done = bf16[512,1024]{1,0:T(8,128)(2,1)S(1)} copy-done((bf16[512,1024]{1,0:T(8,128)(2,1)S(1)}, bf16[512,1024]{1,0:T(8,128)(2,1)}, u32[]{:S(2)}) %copy-start) | copy-done | bytes 1048600
  1.2 3.7 %convolution_convert_fusion = bf16[512,1536]{1,0:T(8,128)(2,1)S(1)} fusion(bf16[512,1024]{1,0:T(8,128)(2,1)S(1)} %copy-done, bf16[1024,1536]{1,0:T(8,128)(2,1)} %param.6), kind=kOutput, calls=%fused_computation.1 | convolution fusion | flops 1611399168 | bytes 5767168 | tf_op jit(solution)/shard_map/dot_general | solution.py:110
  5.8 2.4 %collective-permute-start = (bf16[128,1024]{1,0:T(8,128)(2,1)}, bf16[128,1024]{1,0:T(8,128)(2,1)S(1)}, u32[]{:S(2)}, u32[]{:S(2)}) collective-permute-start(bf16[128,1024]{1,0:T(8,128)(2,1)} %get-tuple-element.8), channel_id=1, source_target_pairs={{0,1},{1,2},{2,3},{3,4},{4,5},{5,6},{6,7},{7,8},{8,9},{9,10},{10,1... | collective-permute-start | bytes 786440 | tf_op jit(solution)/shard_map/ppermute | solution.py:20
  8.1 1.3 %collective-permute-start.1 = (bf16[128,1024]{1,0:T(8,128)(2,1)}, bf16[128,1024]{1,0:T(8,128)(2,1)}, u32[]{:S(2)}, u32[]{:S(2)}) collective-permute-start(bf16[128,1024]{1,0:T(8,128)(2,1)} %get-tuple-element.9), channel_id=1, source_target_pairs={{1,0},{2,1},{3,2},{4,3},{5,4},{6,5},{7,6},{8,7},{9,8},{10,9},{11,1... | collective-permute-start | bytes 786440 | tf_op jit(solution)/shard_map/ppermute | solution.py:22
  9.9 0.9 reshape_reshape.3
  10.8 0.9 fusion.58
  11.7 1.0 %copy.68 = bf16[4,128,512]{1,2,0:T(8,128)(2,1)} copy(bf16[4,128,512]{2,1,0:T(8,128)(2,1)S(1)} %get-tuple-element.13) | data formatting | bytes 1048576 | tf_op jit(solution)/shard_map/slice | solution.py:36
  12.7 45.4 %all-gather = bf16[32,2,1024]{2,1,0:T(2,128)(2,1)S(1)} all-gather(bf16[1,2,1024]{2,1,0:T(2,128)(2,1)S(1)} %bitcast.82), channel_id=1, replica_groups=mesh['grp'=2,'seq'=16] {'grp','seq'}, dimensions={0}, use_global_device_ids=true | all-gather | bytes 135168 | tf_op jit(solution)/shard_map/all_gather | solution.py:115
  58.9 2.2 %fusion.16 = bf16[32,1024]{1,0:T(8,128)(2,1)S(1)} fusion(bf16[1024,1536]{1,0:T(8,128)(2,1)} %param.6, bf16[32,1024]{1,0:T(8,128)(2,1)S(1)} %gather_fusion, pred[32]{0:T(512)(128)(4,1)S(1)} %compare_and_fusion), kind=kOutput, calls=%fused_computation.30 | convolution fusion | flops 67174400 | bytes 2228256 | tf_op jit(solution)/shard_map/dot_general | solution.py:117
  61.7 1.6 %bitcast_reduce_fusion.1 = (f32[4,128,8]{1,2,0:T(8,128)S(1)}, f32[4,8,128,128]{3,2,1,0:T(8,128)S(1)}) fusion(bf16[4,128,8,64]{1,3,2,0:T(8,128)(2,1)S(1)} %bitcast.76, bf16[4,128,8,64]{1,0,3,2:T(4,128)(2,1)} %reshape_reshape.3), kind=kOutput, calls=%fused_computation.6 | convolution fusion | flops 68153344 | bytes 3162112 | tf_op jit(solution)/shard_map/nqhd,nkhd->nqhk/dot_general | solution.py:49
  63.9 2.0 %copy.76 = bf16[4,128,512]{1,2,0:T(8,128)(2,1)} copy(bf16[4,128,512]{2,1,0:T(8,128)(2,1)} %get-tuple-element.12) | data formatting | bytes 1048576 | tf_op jit(solution)/shard_map/slice | solution.py:37
  66.8 2.7 %fusion.61 = (f32[4,128,8]{1,0,2:T(4,128)}, f32[4,128,8,32]{1,3,0,2:T(8,128)}) fusion(bf16[4,128,8,64]{1,0,3,2:T(4,128)(2,1)} %reshape_reshape.3, bf16[32,8,64,1]{2,1,0,3:T(8,128)(2,1)S(1)} %bitcast.81), kind=kOutput, calls=%fused_computation.80 | convolution fusion | flops 17035264 | bytes 1097728 | tf_op jit(solution)/shard_map/nqhd,chd->nqhc/dot_general | solution.py:61
  69.5 2.6 %pad_maximum_fusion.1 = (bf16[512,1024]{1,0:T(8,128)(2,1)S(1)}, bf16[512,1024]{1,0:T(8,128)(2,1)}) fusion(bf16[512,1024]{1,0:T(8,128)(2,1)} %copy-done.3, bf16[128,1024]{1,0:T(8,128)(2,1)S(1)} %collective-permute-done, bf16[128,1024]{1,0:T(8,128)(2,1)} %collective-permute-done.1), kind=kLoop, calls=%fused_computation.33 | loop fusion | flops 4194304 | bytes 3670016 | tf_op jit(solution)/shard_map/concatenate | solution.py:18
  72.1 1.1 %fusion.59 = (bf16[4,128,512]{2,1,0:T(8,128)(2,1)}, bf16[4,128,512]{2,1,0:T(8,128)(2,1)}) fusion(bf16[4,128,1024]{2,1,0:T(8,128)(2,1)S(1)} %bitcast.74), kind=kLoop, calls=%fused_computation.78 | loop fusion | bytes 2097152 | tf_op jit(solution)/shard_map/slice | solution.py:37
  73.2 2.0 %copy.65 = bf16[4,128,512]{1,2,0:T(8,128)(2,1)} copy(bf16[4,128,512]{2,1,0:T(8,128)(2,1)} %get-tuple-element.15) | data formatting | bytes 1048576 | tf_op jit(solution)/shard_map/slice | solution.py:36
  75.3 2.3 %fusion.57 = (bf16[4,128,512]{2,1,0:T(8,128)(2,1)}, bf16[4,128,512]{2,1,0:T(8,128)(2,1)}) fusion(bf16[4,128,1024]{2,1,0:T(8,128)(2,1)} %bitcast.73), kind=kLoop, calls=%fused_computation.76 | loop fusion | bytes 2097152 | tf_op jit(solution)/shard_map/slice | solution.py:37
  77.5 2.1 %copy.70 = bf16[4,128,512]{1,2,0:T(8,128)(2,1)} copy(bf16[4,128,512]{2,1,0:T(8,128)(2,1)} %get-tuple-element.11) | data formatting | bytes 1048576 | tf_op jit(solution)/shard_map/slice | solution.py:36
  79.6 3.3 %bitcast_reduce_fusion.2 = (f32[4,128,8]{1,2,0:T(8,128)S(1)}, f32[4,8,128,128]{3,2,1,0:T(8,128)}) fusion(pred[4]{0:T(512)(128)(4,1)S(1)} %copy-done.11, bf16[4,128,8,64]{1,3,2,0:T(8,128)(2,1)} %bitcast.77, bf16[4,128,8,64]{1,0,3,2:T(4,128)(2,1)} %reshape_reshape.3), kind=kOutput, calls=%fused_computation.9 | convolution fusion | flops 68677632 | bytes 3162116 | tf_op jit(solution)/shard_map/nqhd,nkhd->nqhk/dot_general | solution.py:49
  82.9 2.0 %bitcast_reduce_fusion = (f32[4,128,8]{1,2,0:T(8,128)S(1)}, f32[4,8,128,128]{3,2,1,0:T(8,128)}) fusion(pred[4]{0:T(512)(128)(4,1)S(1)} %copy-done.12, bf16[4,128,8,64]{1,3,2,0:T(8,128)(2,1)S(1)} %bitcast.78, bf16[4,128,8,64]{1,0,3,2:T(4,128)(2,1)S(1)} %copy-done.2), kind=kOutput, calls=%fused_computation.3 | convolution fusion | flops 68677632 | bytes 3162116 | tf_op jit(solution)/shard_map/nqhd,nkhd->nqhk/dot_general | solution.py:49
  84.9 2.0 %copy.64 = bf16[4,128,512]{1,2,0:T(8,128)(2,1)} copy(bf16[4,128,512]{2,1,0:T(8,128)(2,1)} %get-tuple-element.14) | data formatting | bytes 1048576 | tf_op jit(solution)/shard_map/slice | solution.py:37
  86.9 2.1 %copy.78 = bf16[4,128,512]{1,2,0:T(8,128)(2,1)} copy(bf16[4,128,512]{2,1,0:T(8,128)(2,1)} %get-tuple-element.10) | data formatting | bytes 1048576 | tf_op jit(solution)/shard_map/slice | solution.py:37
  89.0 2.6 %fusion.20 = f32[4,8,64,128]{3,2,1,0:T(8,128)S(1)} fusion(bf16[4,128,8,64]{1,3,2,0:T(8,128)(2,1)} %bitcast.79, f32[4,8,128,128]{3,2,1,0:T(8,128)} %get-tuple-element.29, f32[4,128,8]{1,2,0:T(8,128)S(1)} %fusion.49, pred[4]{0:T(512)(128)(4,1)S(1)} %copy-done.11), kind=kOutput, calls=%fused_computation.31 | convolution fusion | flops 69206016 | bytes 3686404 | tf_op jit(solution)/shard_map/nqhk,nkhd->nqhd/dot_general | solution.py:86
  91.6 3.2 %fusion.5 = (f32[4,128,8]{1,2,0:T(8,128)S(1)}, f32[4,128,8]{1,2,0:T(8,128)S(1)}, f32[4,128,8]{1,2,0:T(8,128)S(1)}) fusion(f32[4,8,128,128]{3,2,1,0:T(8,128)S(1)} %get-tuple-element.31, f32[4,128,8]{1,2,0:T(8,128)S(1)} %fusion.49, f32[4,8,128,128]{3,2,1,0:T(8,128)S(1)} %copy-done.1, pred[4]{0:T(512)(128)(4,1)S(1)} %copy-done.11, ...), kind=kLoop, calls=%fused_computation.15 | loop fusion | flops 5754880 | bytes 6357000 | tf_op jit(solution)/shard_map/reduce_sum | solution.py:80
  98.0 1.4 %reshape.105 = bf16[512,512]{1,0:T(8,128)(2,1)} reshape(bf16[4,128,8,64]{3,2,1,0:T(8,128)(2,1)S(1)} %copy.92) | data formatting | bytes 1048576 | tf_op jit(solution)/shard_map/reshape | solution.py:102
  (54 shorter events, 7.3 us)
Async XLA Ops:
  0.0 1.2 %copy-start = (bf16[512,1024]{1,0:T(8,128)(2,1)S(1)}, bf16[512,1024]{1,0:T(8,128)(2,1)}, u32[]{:S(2)}) copy-start(bf16[512,1024]{1,0:T(8,128)(2,1)} %param.5) | copy-start | bytes 3145732
  4.9 4.7 %copy-start.15 = (s32[32]{0:T(128)S(1)}, s32[32]{0:T(128)}, u32[]{:S(2)}) copy-start(s32[32]{0:T(128)} %param.8) | copy-start | bytes 388
  5.8 63.7 %collective-permute-start = (bf16[128,1024]{1,0:T(8,128)(2,1)}, bf16[128,1024]{1,0:T(8,128)(2,1)S(1)}, u32[]{:S(2)}, u32[]{:S(2)}) collective-permute-start(bf16[128,1024]{1,0:T(8,128)(2,1)} %get-tuple-element.8), channel_id=1, source_target_pairs={{0,1},{1,2},{2,3},{3,4},{4,5},{5,6},{6,7},{7,8},{8,9},{9,10},{10,1... | collective-permute-start | bytes 786440 | tf_op jit(solution)/shard_map/ppermute | solution.py:20
  8.1 61.4 %collective-permute-start.1 = (bf16[128,1024]{1,0:T(8,128)(2,1)}, bf16[128,1024]{1,0:T(8,128)(2,1)}, u32[]{:S(2)}, u32[]{:S(2)}) collective-permute-start(bf16[128,1024]{1,0:T(8,128)(2,1)} %get-tuple-element.9), channel_id=1, source_target_pairs={{1,0},{2,1},{3,2},{4,3},{5,4},{6,5},{7,6},{8,7},{9,8},{10,9},{11,1... | collective-permute-start | bytes 786440 | tf_op jit(solution)/shard_map/ppermute | solution.py:22
  9.6 2.2 %copy-start.3 = (bf16[512,1024]{1,0:T(8,128)(2,1)}, bf16[512,1024]{1,0:T(8,128)(2,1)S(1)}, u32[]{:S(2)}) copy-start(bf16[512,1024]{1,0:T(8,128)(2,1)S(1)} %slice.75) | copy-start | bytes 3145732
  9.9 2.8 %copy-start.13 = (bf16[2,1024]{1,0:T(2,128)(2,1)S(1)}, bf16[2,1024]{1,0:T(2,128)(2,1)}, u32[]{:S(2)}) copy-start(bf16[2,1024]{1,0:T(2,128)(2,1)} %param.7) | copy-start | bytes 12292
  58.9 2.8 %copy-start.7 = (bf16[4,128,512]{1,2,0:T(8,128)(2,1)S(1)}, bf16[4,128,512]{1,2,0:T(8,128)(2,1)}, u32[]{:S(2)}) copy-start(bf16[4,128,512]{1,2,0:T(8,128)(2,1)} %copy.68) | copy-start | bytes 1572868
  61.1 2.2 %copy-start.14 = (s32[4,2]{0,1:T(2,128)S(1)}, s32[4,2]{0,1:T(2,128)}, u32[]{:S(2)}) copy-start(s32[4,2]{0,1:T(2,128)} %param.9) | copy-start | bytes 100
  73.2 6.4 %copy-start.11 = (pred[4]{0:T(512)(128)(4,1)S(1)}, pred[4]{0:T(512)(128)(4,1)}, u32[]{:S(2)}) copy-start(pred[4]{0:T(512)(128)(4,1)} %get-tuple-element.22) | copy-start | bytes 16
  77.5 5.3 %copy-start.12 = (pred[4]{0:T(512)(128)(4,1)S(1)}, pred[4]{0:T(512)(128)(4,1)}, u32[]{:S(2)}) copy-start(pred[4]{0:T(512)(128)(4,1)} %get-tuple-element.23) | copy-start | bytes 16
  79.6 3.3 %copy-start.2 = (bf16[4,128,8,64]{1,0,3,2:T(4,128)(2,1)S(1)}, bf16[4,128,8,64]{1,0,3,2:T(4,128)(2,1)}, u32[]{:S(2)}) copy-start(bf16[4,128,8,64]{1,0,3,2:T(4,128)(2,1)} %reshape_reshape.3) | copy-start | bytes 1572868
  79.6 3.3 %copy-start.8 = (bf16[4,128,512]{1,2,0:T(8,128)(2,1)S(1)}, bf16[4,128,512]{1,2,0:T(8,128)(2,1)}, u32[]{:S(2)}) copy-start(bf16[4,128,512]{1,2,0:T(8,128)(2,1)} %copy.70) | copy-start | bytes 1572868
  82.9 2.0 %copy-start.10 = (f32[4,128,8]{1,0,2:T(4,128)S(1)}, f32[4,128,8]{1,0,2:T(4,128)}, u32[]{:S(2)}) copy-start(f32[4,128,8]{1,0,2:T(4,128)} %get-tuple-element.26) | copy-start | bytes 49156
  89.0 2.6 %copy-start.1 = (f32[4,8,128,128]{3,2,1,0:T(8,128)S(1)}, f32[4,8,128,128]{3,2,1,0:T(8,128)}, u32[]{:S(2)}) copy-start(f32[4,8,128,128]{3,2,1,0:T(8,128)} %get-tuple-element.29) | copy-start | bytes 6291460
  91.6 3.2 %copy-start.6 = (f32[4,128,8,32]{1,3,0,2:T(8,128)S(1)}, f32[4,128,8,32]{1,3,0,2:T(8,128)}, u32[]{:S(2)}) copy-start(f32[4,128,8,32]{1,3,0,2:T(8,128)} %get-tuple-element.27) | copy-start | bytes 1572868
  91.6 3.4 %copy-start.5 = (bf16[4,128,512]{1,2,0:T(8,128)(2,1)S(1)}, bf16[4,128,512]{1,2,0:T(8,128)(2,1)}, u32[]{:S(2)}) copy-start(bf16[4,128,512]{1,2,0:T(8,128)(2,1)} %copy.76) | copy-start | bytes 1572868
  95.0 1.6 %copy-start.4 = (f32[4,8,128,128]{3,2,1,0:T(8,128)S(1)}, f32[4,8,128,128]{3,2,1,0:T(8,128)}, u32[]{:S(2)}) copy-start(f32[4,8,128,128]{3,2,1,0:T(8,128)} %get-tuple-element.25) | copy-start | bytes 6291460
  95.0 1.7 %copy-start.9 = (bf16[4,128,512]{1,2,0:T(8,128)(2,1)S(1)}, bf16[4,128,512]{1,2,0:T(8,128)(2,1)}, u32[]{:S(2)}) copy-start(bf16[4,128,512]{1,2,0:T(8,128)(2,1)} %copy.78) | copy-start | bytes 1572868
where the time goes:
time: 100 us; the launch traced here: 99.4 us
  blocking collectives  45.4 us (45%)
  local copies, waits for them, and re-layouts  24 us (24%)
  matrix products  19.6 us (20%)
  other arithmetic  6.55 us (7%)
  starting transfers between devices  3.65 us (4%)
    all_gather x1, blocking collectives, local(): every_row = lax.all_gather(cov_embed, ('grp', 'seq'), axis=0, tiled=True)  45.4 us
    slice x6, local copies, waits for them, and re-layouts, divide_parts(): joined[:, :, attn_width:]  10.4 us
    dot_general x3, matrix products, local_scores(): jnp.einsum('nqhd,nkhd->nqhk', query_heads, key_part, preferred_element_ty...  6.79 us
    slice x3, local copies, waits for them, and re-layouts, divide_parts(): joined[:, :, :attn_width]  5.1 us
    dot_general x3, matrix products, local_values(): jnp.einsum('nqhk,nkhd->nqhd', weights.astype(jnp.bfloat16), value_part, p...  3.93 us
    dot_general x1, matrix products, local(): jnp.dot(tokens, qkv_weight, preferred_element_type=jnp.float32)  3.67 us
    reduce_sum x1, other arithmetic, window_attend(): jnp.sum(weight_middle, axis=-1)  3.2 us
    dot_general x1, matrix products, window_attend(): jnp.einsum('nqhd,chd->nqhc', query_heads, cov_keys, preferred_element_typ...  2.66 us
  transfers between devices with their start and end apart: 2, of which 0 were waited for; matrix products, arithmetic and copies ran while one was open for 15% of the time, Pallas kernels for 0%

commit v1 on v0

--- a/solution.py
+++ b/solution.py
@@ -7,6 +7,29 @@
 HEADS = 8
 BLOCK = 128
 masked_score = -1e30
+
+
+def laid_out(blocks, dim):
+    lengths = list(blocks.shape[1:])
+    lengths[dim] *= blocks.shape[0]
+    return jnp.moveaxis(blocks, 0, dim).reshape(lengths)
+
+
+def collected_by_bits(x, axis):
+    devices, mine = (lax.axis_size(axis), lax.axis_index(axis))
+    blocks, bit = (x[None], 1)
+    while bit < devices:
+        partner_block = lax.ppermute(blocks, axis, [(i, i ^ bit) for i in range(devices)])
+        low = mine & bit == 0
+        blocks = jnp.concatenate(
+            [jnp.where(low, blocks, partner_block), jnp.where(low, partner_block, blocks)]
+        )
+        bit *= 2
+    return blocks
+
+
+def doubled_up(x, axis, dim):
+    return laid_out(collected_by_bits(x, axis), dim)
 
 
 def extended(cells, sides, width):
@@ -112,7 +135,7 @@
     keyvalue = projected[:, attn_width:]
     padded = extended(keyvalue, ((("grp", "seq"), 0),), block_rows)
     value_weight = qkv_weight[:, attn_width:]
-    every_row = lax.all_gather(cov_embed, ("grp", "seq"), axis=0, tiled=True)
+    every_row = doubled_up(cov_embed, ("grp", "seq"), 0)
     chosen = jnp.take(every_row, cov_slot, axis=0)
     cov_kv = jnp.dot(chosen, value_weight, preferred_element_type=jnp.float32).astype(jnp.bfloat16)
     before = padded[:tok_rows].reshape(blocks, block_rows, 2 * attn_width)

time: 100 us -> 74.1 us (0.74)
  blocking collectives: 45.4 us -> 0 us
  starting transfers between devices: 3.65 us -> 19.6 us
  waiting for transfers between devices: 0.01 us -> 5.58 us
  local copies, waits for them, and re-layouts: 24 us -> 22.2 us
    all_gather x1 -> x0, blocking collectives: 45.4 us -> none  [local(): every_row = lax.all_gather(cov_embed, ('grp', 'seq'), axis=0, tiled=True)]
    ppermute x0 -> x5, starting transfers between devices: none -> 15.3 us  [collected_by_bits(): lax.ppermute(blocks, axis, [(i, i ^ bit) for i in range(devices)])]
    ppermute x0 -> x5, waiting for transfers between devices: none -> 5.57 us  [collected_by_bits(): lax.ppermute(blocks, axis, [(i, i ^ bit) for i in range(devices)])]
    unnamed x33 -> x24, local copies, waits for them, and re-layouts: 2.14 us -> 1.6 us
  transfers between devices with their start and end apart: 2 -> 7, of which waited for: 0 -> 3; matrix products, arithmetic and copies ran while one was open for 15% -> 24% of each run, Pallas kernels for 0% -> 0%
where the time goes in v1:
time: 74.1 us; the launch traced here: 73.5 us
  local copies, waits for them, and re-layouts  22.2 us (30%)
  starting transfers between devices  19.6 us (26%)
  matrix products  19 us (26%)
  other arithmetic  6.73 us (9%)
  waiting for transfers between devices  5.58 us (8%)
    ppermute x5, starting transfers between devices, collected_by_bits(): lax.ppermute(blocks, axis, [(i, i ^ bit) for i in range(devices)])  15.3 us
    slice x6, local copies, waits for them, and re-layouts, divide_parts(): joined[:, :, attn_width:]  10.5 us
    dot_general x3, matrix products, local_scores(): jnp.einsum('nqhd,nkhd->nqhk', query_heads, key_part, preferred_element_ty...  6.93 us
    ppermute x5, waiting for transfers between devices, collected_by_bits(): lax.ppermute(blocks, axis, [(i, i ^ bit) for i in range(devices)])  5.57 us
    slice x3, local copies, waits for them, and re-layouts, divide_parts(): joined[:, :, :attn_width]  5.13 us
    dot_general x3, matrix products, local_values(): jnp.einsum('nqhk,nkhd->nqhd', weights.astype(jnp.bfloat16), value_part, p...  3.93 us
    dot_general x1, matrix products, local(): jnp.dot(tokens, qkv_weight, preferred_element_type=jnp.float32)  3.67 us
    reduce_sum x1, other arithmetic, window_attend(): jnp.sum(weight_middle, axis=-1)  3.2 us
  transfers between devices with their start and end apart: 7, of which 3 were waited for; matrix products, arithmetic and copies ran while one was open for 24% of the time, Pallas kernels for 0%

profile of v1, /device:TPU:0, one launch (start us, length us, event | category | flops | bytes accessed | tf_op | source)
XLA Modules:
  0.0 73.5 jit_solution(7730554411755718641)
XLA Ops:
  1.2 3.7 %convolution_convert_fusion = bf16[512,1536]{1,0:T(8,128)(2,1)S(1)} fusion(bf16[512,1024]{1,0:T(8,128)(2,1)S(1)} %copy-done, bf16[1024,1536]{1,0:T(8,128)(2,1)} %param.6), kind=kOutput, calls=%fused_computation.1 | convolution fusion | flops 1611399168 | bytes 5767168 | tf_op jit(solution)/shard_map/dot_general | solution.py:133
  5.8 3.0 %collective-permute-start = (bf16[128,1024]{1,0:T(8,128)(2,1)}, bf16[128,1024]{1,0:T(8,128)(2,1)}, u32[]{:S(2)}, u32[]{:S(2)}) collective-permute-start(bf16[128,1024]{1,0:T(8,128)(2,1)} %get-tuple-element.8), channel_id=1, source_target_pairs={{0,1},{1,2},{2,3},{3,4},{4,5},{5,6},{6,7},{7,8},{8,9},{9,10},{10,1... | collective-permute-start | bytes 786440 | tf_op jit(solution)/shard_map/ppermute | solution.py:43
  13.4 1.7 %bitcast_reduce_fusion.1 = (f32[4,128,8]{1,2,0:T(8,128)S(1)}, f32[4,8,128,128]{3,2,1,0:T(8,128)S(1)}) fusion(bf16[4,128,8,64]{1,3,2,0:T(8,128)(2,1)} %bitcast.81, bf16[4,128,8,64]{1,0,3,2:T(4,128)(2,1)} %reshape_reshape.3), kind=kOutput, calls=%fused_computation.6 | convolution fusion | flops 68153344 | bytes 3162112 | tf_op jit(solution)/shard_map/nqhd,nkhd->nqhk/dot_general | solution.py:72
  15.2 4.3 %collective-permute-start.3 = (bf16[2,2,1024]{2,1,0:T(2,128)(2,1)S(1)}, bf16[2,2,1024]{2,1,0:T(2,128)(2,1)S(1)}, u32[]{:S(2)}, u32[]{:S(2)}) collective-permute-start(bf16[2,2,1024]{2,1,0:T(2,128)(2,1)S(1)} %pad_maximum_fusion.6), channel_id=1, source_target_pairs={{0,2},{1,3},{2,0},{3,1},{4,6},{5,7},{6,4},{7,5},{8,10},{9,11},{10,... | collective-permute-start | bytes 24584 | tf_op jit(solution)/shard_map/ppermute | solution.py:22
  19.5 1.6 %collective-permute-done.3 = bf16[2,2,1024]{2,1,0:T(2,128)(2,1)S(1)} collective-permute-done((bf16[2,2,1024]{2,1,0:T(2,128)(2,1)S(1)}, bf16[2,2,1024]{2,1,0:T(2,128)(2,1)S(1)}, u32[]{:S(2)}, u32[]{:S(2)}) %collective-permute-start.3) | collective-permute-done | bytes 8224 | tf_op jit(solution)/shard_map/ppermute | solution.py:22
  21.2 3.0 %collective-permute-start.4 = (bf16[4,2,1024]{2,1,0:T(2,128)(2,1)S(1)}, bf16[4,2,1024]{2,1,0:T(2,128)(2,1)S(1)}, u32[]{:S(2)}, u32[]{:S(2)}) collective-permute-start(bf16[4,2,1024]{2,1,0:T(2,128)(2,1)S(1)} %pad_maximum_fusion.5), channel_id=1, source_target_pairs={{0,4},{1,5},{2,6},{3,7},{4,0},{5,1},{6,2},{7,3},{8,12},{9,13},{10,... | collective-permute-start | bytes 49160 | tf_op jit(solution)/shard_map/ppermute | solution.py:22
  24.2 1.7 %collective-permute-done.4 = bf16[4,2,1024]{2,1,0:T(2,128)(2,1)S(1)} collective-permute-done((bf16[4,2,1024]{2,1,0:T(2,128)(2,1)S(1)}, bf16[4,2,1024]{2,1,0:T(2,128)(2,1)S(1)}, u32[]{:S(2)}, u32[]{:S(2)}) %collective-permute-start.4) | collective-permute-done | bytes 16416 | tf_op jit(solution)/shard_map/ppermute | solution.py:22
  26.0 3.1 %collective-permute-start.5 = (bf16[8,2,1024]{2,1,0:T(2,128)(2,1)S(1)}, bf16[8,2,1024]{2,1,0:T(2,128)(2,1)S(1)}, u32[]{:S(2)}, u32[]{:S(2)}) collective-permute-start(bf16[8,2,1024]{2,1,0:T(2,128)(2,1)S(1)} %pad_maximum_fusion.4), channel_id=1, source_target_pairs={{0,8},{1,9},{2,10},{3,11},{4,12},{5,13},{6,14},{7,15},{8,0},{9,1},... | collective-permute-start | bytes 98312 | tf_op jit(solution)/shard_map/ppermute | solution.py:22
  29.1 2.0 %copy.76 = bf16[4,128,512]{1,2,0:T(8,128)(2,1)} copy(bf16[4,128,512]{2,1,0:T(8,128)(2,1)} %get-tuple-element.12) | data formatting | bytes 1048576 | tf_op jit(solution)/shard_map/slice | solution.py:60
  31.4 4.4 %collective-permute-start.6 = (bf16[16,2,1024]{2,1,0:T(2,128)(2,1)S(1)}, bf16[16,2,1024]{2,1,0:T(2,128)(2,1)S(1)}, u32[]{:S(2)}, u32[]{:S(2)}) collective-permute-start(bf16[16,2,1024]{2,1,0:T(2,128)(2,1)S(1)} %pad_maximum_fusion.3), channel_id=1, source_target_pairs={{0,16},{1,17},{2,18},{3,19},{4,20},{5,21},{6,22},{7,23},{8,24},{9,... | collective-permute-start | bytes 196616 | tf_op jit(solution)/shard_map/ppermute | solution.py:22
  35.8 2.2 %collective-permute-done.6 = bf16[16,2,1024]{2,1,0:T(2,128)(2,1)S(1)} collective-permute-done((bf16[16,2,1024]{2,1,0:T(2,128)(2,1)S(1)}, bf16[16,2,1024]{2,1,0:T(2,128)(2,1)S(1)}, u32[]{:S(2)}, u32[]{:S(2)}) %collective-permute-start.6) | collective-permute-done | bytes 65568 | tf_op jit(solution)/shard_map/ppermute | solution.py:22
  39.1 2.1 %fusion.16 = bf16[32,1024]{1,0:T(8,128)(2,1)S(1)} fusion(bf16[1024,1536]{1,0:T(8,128)(2,1)} %param.6, bf16[32,1024]{1,0:T(8,128)(2,1)S(1)} %gather_fusion, pred[32]{0:T(512)(128)(4,1)S(1)} %compare_and_fusion), kind=kOutput, calls=%fused_computation.30 | convolution fusion | flops 67174400 | bytes 2228256 | tf_op jit(solution)/shard_map/dot_general | solution.py:140
  41.4 2.1 %fusion.61 = (f32[4,128,8]{1,0,2:T(4,128)S(1)}, f32[4,128,8,32]{1,3,0,2:T(8,128)}) fusion(bf16[4,128,8,64]{1,0,3,2:T(4,128)(2,1)} %reshape_reshape.3, bf16[32,8,64,1]{2,1,0,3:T(8,128)(2,1)S(1)} %bitcast.83), kind=kOutput, calls=%fused_computation.95 | convolution fusion | flops 17035264 | bytes 1097728 | tf_op jit(solution)/shard_map/nqhd,chd->nqhc/dot_general | solution.py:84
  43.5 2.7 %pad_maximum_fusion.1 = (bf16[512,1024]{1,0:T(8,128)(2,1)S(1)}, bf16[512,1024]{1,0:T(8,128)(2,1)}) fusion(bf16[512,1024]{1,0:T(8,128)(2,1)} %copy-done.3, bf16[128,1024]{1,0:T(8,128)(2,1)} %collective-permute-done, bf16[128,1024]{1,0:T(8,128)(2,1)} %collective-permute-done.1), kind=kLoop, calls=%fused_computation.33 | loop fusion | flops 4194304 | bytes 3670016 | tf_op jit(solution)/shard_map/concatenate | solution.py:41
  47.3 2.0 %copy.65 = bf16[4,128,512]{1,2,0:T(8,128)(2,1)} copy(bf16[4,128,512]{2,1,0:T(8,128)(2,1)} %get-tuple-element.15) | data formatting | bytes 1048576 | tf_op jit(solution)/shard_map/slice | solution.py:59
  49.3 2.2 %fusion.57 = (bf16[4,128,512]{2,1,0:T(8,128)(2,1)}, bf16[4,128,512]{2,1,0:T(8,128)(2,1)}) fusion(bf16[4,128,1024]{2,1,0:T(8,128)(2,1)} %bitcast.75), kind=kLoop, calls=%fused_computation.91 | loop fusion | bytes 2097152 | tf_op jit(solution)/shard_map/slice | solution.py:60
  51.5 2.1 %copy.70 = bf16[4,128,512]{1,2,0:T(8,128)(2,1)} copy(bf16[4,128,512]{2,1,0:T(8,128)(2,1)} %get-tuple-element.11) | data formatting | bytes 1048576 | tf_op jit(solution)/shard_map/slice | solution.py:59
  53.6 3.2 %bitcast_reduce_fusion.2 = (f32[4,128,8]{1,2,0:T(8,128)S(1)}, f32[4,8,128,128]{3,2,1,0:T(8,128)}) fusion(pred[4]{0:T(512)(128)(4,1)S(1)} %get-tuple-element.32, bf16[4,128,8,64]{1,3,2,0:T(8,128)(2,1)} %bitcast.78, bf16[4,128,8,64]{1,0,3,2:T(4,128)(2,1)} %reshape_reshape.3), kind=kOutput, calls=%fused_computation.9 | convolution fusion | flops 68677632 | bytes 3162116 | tf_op jit(solution)/shard_map/nqhd,nkhd->nqhk/dot_general | solution.py:72
  56.9 2.0 %bitcast_reduce_fusion = (f32[4,128,8]{1,2,0:T(8,128)S(1)}, f32[4,8,128,128]{3,2,1,0:T(8,128)}) fusion(pred[4]{0:T(512)(128)(4,1)S(1)} %get-tuple-element.33, bf16[4,128,8,64]{1,3,2,0:T(8,128)(2,1)S(1)} %bitcast.79, bf16[4,128,8,64]{1,0,3,2:T(4,128)(2,1)S(1)} %copy-done.2), kind=kOutput, calls=%fused_computation.3 | convolution fusion | flops 68677632 | bytes 3162116 | tf_op jit(solution)/shard_map/nqhd,nkhd->nqhk/dot_general | solution.py:72
  58.9 2.0 %copy.64 = bf16[4,128,512]{1,2,0:T(8,128)(2,1)} copy(bf16[4,128,512]{2,1,0:T(8,128)(2,1)} %get-tuple-element.14) | data formatting | bytes 1048576 | tf_op jit(solution)/shard_map/slice | solution.py:60
  60.9 2.1 %copy.78 = bf16[4,128,512]{1,2,0:T(8,128)(2,1)} copy(bf16[4,128,512]{2,1,0:T(8,128)(2,1)} %get-tuple-element.10) | data formatting | bytes 1048576 | tf_op jit(solution)/shard_map/slice | solution.py:60
  63.0 2.6 %fusion.20 = f32[4,8,64,128]{3,2,1,0:T(8,128)S(1)} fusion(bf16[4,128,8,64]{1,3,2,0:T(8,128)(2,1)} %bitcast.80, f32[4,8,128,128]{3,2,1,0:T(8,128)} %get-tuple-element.39, f32[4,128,8]{1,2,0:T(8,128)S(1)} %fusion.49, pred[4]{0:T(512)(128)(4,1)S(1)} %get-tuple-element.32), kind=kOutput, calls=%fused_computation.31 | convolution fusion | flops 69206016 | bytes 3686404 | tf_op jit(solution)/shard_map/nqhk,nkhd->nqhd/dot_general | solution.py:109
  65.6 3.2 %fusion.5 = (f32[4,128,8]{1,2,0:T(8,128)S(1)}, f32[4,128,8]{1,2,0:T(8,128)S(1)}, f32[4,128,8]{1,2,0:T(8,128)S(1)}) fusion(f32[4,8,128,128]{3,2,1,0:T(8,128)S(1)} %get-tuple-element.41, f32[4,128,8]{1,2,0:T(8,128)S(1)} %fusion.49, f32[4,8,128,128]{3,2,1,0:T(8,128)S(1)} %copy-done.1, pred[4]{0:T(512)(128)(4,1)S(1)} %get-tuple-element.32, ...), kind=kLoop, calls=%fused_computation.15 | loop fusion | flops 5754880 | bytes 6357000 | tf_op jit(solution)/shard_map/reduce_sum | solution.py:103
  72.0 1.4 %reshape.107 = bf16[512,512]{1,0:T(8,128)(2,1)} reshape(bf16[4,128,8,64]{3,2,1,0:T(8,128)(2,1)S(1)} %copy.92) | data formatting | bytes 1048576 | tf_op jit(solution)/shard_map/reshape | solution.py:125
  (65 shorter events, 12.6 us)
Async XLA Ops:
  0.0 1.2 %copy-start = (bf16[512,1024]{1,0:T(8,128)(2,1)S(1)}, bf16[512,1024]{1,0:T(8,128)(2,1)}, u32[]{:S(2)}) copy-start(bf16[512,1024]{1,0:T(8,128)(2,1)} %param.5) | copy-start | bytes 3145732
  0.0 15.1 %collective-permute-start.2 = (bf16[1,2,1024]{2,1,0:T(2,128)(2,1)}, bf16[1,2,1024]{2,1,0:T(2,128)(2,1)S(1)}, u32[]{:S(2)}, u32[]{:S(2)}) collective-permute-start(bf16[1,2,1024]{2,1,0:T(2,128)(2,1)} %bitcast.84), channel_id=1, source_target_pairs={{0,1},{1,0},{2,3},{3,2},{4,5},{5,4},{6,7},{7,6},{8,9},{9,8},{10,11... | collective-permute-start | bytes 12296 | tf_op jit(solution)/shard_map/ppermute | solution.py:22
  5.8 37.7 %collective-permute-start = (bf16[128,1024]{1,0:T(8,128)(2,1)}, bf16[128,1024]{1,0:T(8,128)(2,1)}, u32[]{:S(2)}, u32[]{:S(2)}) collective-permute-start(bf16[128,1024]{1,0:T(8,128)(2,1)} %get-tuple-element.8), channel_id=1, source_target_pairs={{0,1},{1,2},{2,3},{3,4},{4,5},{5,6},{6,7},{7,8},{8,9},{9,10},{10,1... | collective-permute-start | bytes 786440 | tf_op jit(solution)/shard_map/ppermute | solution.py:43
  8.8 34.6 %collective-permute-start.1 = (bf16[128,1024]{1,0:T(8,128)(2,1)}, bf16[128,1024]{1,0:T(8,128)(2,1)}, u32[]{:S(2)}, u32[]{:S(2)}) collective-permute-start(bf16[128,1024]{1,0:T(8,128)(2,1)} %get-tuple-element.9), channel_id=1, source_target_pairs={{1,0},{2,1},{3,2},{4,3},{5,4},{6,5},{7,6},{8,7},{9,8},{10,9},{11,1... | collective-permute-start | bytes 786440 | tf_op jit(solution)/shard_map/ppermute | solution.py:45
  10.3 2.1 %copy-start.3 = (bf16[512,1024]{1,0:T(8,128)(2,1)}, bf16[512,1024]{1,0:T(8,128)(2,1)S(1)}, u32[]{:S(2)}) copy-start(bf16[512,1024]{1,0:T(8,128)(2,1)S(1)} %slice.75) | copy-start | bytes 3145732
  12.4 2.8 %copy-start.9 = (bf16[2,1024]{1,0:T(2,128)(2,1)S(1)}, bf16[2,1024]{1,0:T(2,128)(2,1)}, u32[]{:S(2)}) copy-start(bf16[2,1024]{1,0:T(2,128)(2,1)} %param.7) | copy-start | bytes 12292
  12.4 7.1 %copy-start.10 = (s32[4,2]{0,1:T(2,128)S(1)}, s32[4,2]{0,1:T(2,128)}, u32[]{:S(2)}) copy-start(s32[4,2]{0,1:T(2,128)} %param.9) | copy-start | bytes 100
  12.4 11.8 %copy-start.11 = (s32[32]{0:T(128)S(1)}, s32[32]{0:T(128)}, u32[]{:S(2)}) copy-start(s32[32]{0:T(128)} %param.8) | copy-start | bytes 388
  15.2 5.9 %collective-permute-start.3 = (bf16[2,2,1024]{2,1,0:T(2,128)(2,1)S(1)}, bf16[2,2,1024]{2,1,0:T(2,128)(2,1)S(1)}, u32[]{:S(2)}, u32[]{:S(2)}) collective-permute-start(bf16[2,2,1024]{2,1,0:T(2,128)(2,1)S(1)} %pad_maximum_fusion.6), channel_id=1, source_target_pairs={{0,2},{1,3},{2,0},{3,1},{4,6},{5,7},{6,4},{7,5},{8,10},{9,11},{10,... | collective-permute-start | bytes 24584 | tf_op jit(solution)/shard_map/ppermute | solution.py:22
  21.2 4.8 %collective-permute-start.4 = (bf16[4,2,1024]{2,1,0:T(2,128)(2,1)S(1)}, bf16[4,2,1024]{2,1,0:T(2,128)(2,1)S(1)}, u32[]{:S(2)}, u32[]{:S(2)}) collective-permute-start(bf16[4,2,1024]{2,1,0:T(2,128)(2,1)S(1)} %pad_maximum_fusion.5), channel_id=1, source_target_pairs={{0,4},{1,5},{2,6},{3,7},{4,0},{5,1},{6,2},{7,3},{8,12},{9,13},{10,... | collective-permute-start | bytes 49160 | tf_op jit(solution)/shard_map/ppermute | solution.py:22
  26.0 5.1 %collective-permute-start.5 = (bf16[8,2,1024]{2,1,0:T(2,128)(2,1)S(1)}, bf16[8,2,1024]{2,1,0:T(2,128)(2,1)S(1)}, u32[]{:S(2)}, u32[]{:S(2)}) collective-permute-start(bf16[8,2,1024]{2,1,0:T(2,128)(2,1)S(1)} %pad_maximum_fusion.4), channel_id=1, source_target_pairs={{0,8},{1,9},{2,10},{3,11},{4,12},{5,13},{6,14},{7,15},{8,0},{9,1},... | collective-permute-start | bytes 98312 | tf_op jit(solution)/shard_map/ppermute | solution.py:22
  31.4 6.7 %collective-permute-start.6 = (bf16[16,2,1024]{2,1,0:T(2,128)(2,1)S(1)}, bf16[16,2,1024]{2,1,0:T(2,128)(2,1)S(1)}, u32[]{:S(2)}, u32[]{:S(2)}) collective-permute-start(bf16[16,2,1024]{2,1,0:T(2,128)(2,1)S(1)} %pad_maximum_fusion.3), channel_id=1, source_target_pairs={{0,16},{1,17},{2,18},{3,19},{4,20},{5,21},{6,22},{7,23},{8,24},{9,... | collective-permute-start | bytes 196616 | tf_op jit(solution)/shard_map/ppermute | solution.py:22
  53.6 3.2 %copy-start.2 = (bf16[4,128,8,64]{1,0,3,2:T(4,128)(2,1)S(1)}, bf16[4,128,8,64]{1,0,3,2:T(4,128)(2,1)}, u32[]{:S(2)}) copy-start(bf16[4,128,8,64]{1,0,3,2:T(4,128)(2,1)} %reshape_reshape.3) | copy-start | bytes 1572868
  53.6 3.2 %copy-start.7 = (bf16[4,128,512]{1,2,0:T(8,128)(2,1)S(1)}, bf16[4,128,512]{1,2,0:T(8,128)(2,1)}, u32[]{:S(2)}) copy-start(bf16[4,128,512]{1,2,0:T(8,128)(2,1)} %copy.70) | copy-start | bytes 1572868
  63.0 2.6 %copy-start.1 = (f32[4,8,128,128]{3,2,1,0:T(8,128)S(1)}, f32[4,8,128,128]{3,2,1,0:T(8,128)}, u32[]{:S(2)}) copy-start(f32[4,8,128,128]{3,2,1,0:T(8,128)} %get-tuple-element.39) | copy-start | bytes 6291460
  65.6 3.2 %copy-start.6 = (f32[4,128,8,32]{1,3,0,2:T(8,128)S(1)}, f32[4,128,8,32]{1,3,0,2:T(8,128)}, u32[]{:S(2)}) copy-start(f32[4,128,8,32]{1,3,0,2:T(8,128)} %get-tuple-element.37) | copy-start | bytes 1572868
  65.6 3.4 %copy-start.5 = (bf16[4,128,512]{1,2,0:T(8,128)(2,1)S(1)}, bf16[4,128,512]{1,2,0:T(8,128)(2,1)}, u32[]{:S(2)}) copy-start(bf16[4,128,512]{1,2,0:T(8,128)(2,1)} %copy.76) | copy-start | bytes 1572868
  69.0 1.6 %copy-start.4 = (f32[4,8,128,128]{3,2,1,0:T(8,128)S(1)}, f32[4,8,128,128]{3,2,1,0:T(8,128)}, u32[]{:S(2)}) copy-start(f32[4,8,128,128]{3,2,1,0:T(8,128)} %get-tuple-element.35) | copy-start | bytes 6291460
  69.0 1.7 %copy-start.8 = (bf16[4,128,512]{1,2,0:T(8,128)(2,1)S(1)}, bf16[4,128,512]{1,2,0:T(8,128)(2,1)}, u32[]{:S(2)}) copy-start(bf16[4,128,512]{1,2,0:T(8,128)(2,1)} %copy.78) | copy-start | bytes 1572868
